TPU v7x, 32 devices: a whole 2x2x4 slice. The times are simulated.
32 devices in a mesh: tm: 16 (over z, y, x), rows: 2 (over core).
Axes of the slice: x: 2, y: 2, z: 4, core: 2. Of those that a mesh axis runs over, the one named last changes fastest.
Arguments:
- band_blocks: float32 [8, 3, 64, 64], replicated, may hold values from 0.1 to 1
- band_offsets: int32 [8, 3], replicated, may hold values from 0 to 7, as said below
- retention: float32 [512], replicated, may hold values from 0.85 to 0.99
- frame_scale: float32 [64, 8], P('tm'), may hold values from 0.95 to 0.999
- sensor_index: int32 [128], replicated, may hold values from 0 to 511, as said below
- sensor_gain: float32 [128], replicated, may hold values from 0.2 to 0.6
- readings: float32 [64, 128], P('tm'), may hold values from -6 to 6
- noise_cov: float32 [512, 512], P(None, 'rows'), may hold values from -0.01 to 0.2
- initial_mean: float32 [512], replicated, may hold values from -6 to 6
- smoother_gain: float32 [512, 512], replicated, may hold values from -0.001 to 1, as said below
Outputs:
- filtered_cov: float32 [16, 512, 512], P('tm', None, 'rows')
- smoothed_means: float32 [64, 512], P('tm', 'rows')
Inputs may be any that keep to these rules, and one draw needn't show every extreme that they name: `band_offsets`: band 0 of block row i names block i; the other bands of a row name distinct other blocks. `sensor_index`: the sensors read distinct nodes. Every eigenvalue of smoother_gain lies inside the unit circle.
All inputs are finite; a program needn't handle non-finite values.
Results may differ from a plain program's by a relative error of at most 0.0003.
Values sent between devices are 32-bit elements; how exact they have to be, the bound alone decides.
A program may use at most 64 MiB of HBM per device.

v0:
```python
import functools

import jax
import jax.numpy as jnp
from jax import lax
from jax.experimental import pallas as pl
from jax.experimental.pallas import tpu as pltpu
from jax.sharding import PartitionSpec as P

F32 = jnp.float32
BF16 = jnp.bfloat16
NT = (((1,), (1,)), ((), ()))


def dot(left, right):
    return jnp.dot(left, right, preferred_element_type=F32)


def dot_nt(left, right):
    return lax.dot_general(left, right, NT, preferred_element_type=F32)


def split(value):
    high = value.astype(BF16)
    return high, (value - high.astype(F32)).astype(BF16)


def column(row, width=128):
    return jnp.transpose(jnp.broadcast_to(row, (width, row.shape[1])))


def kernel(
    where_ref, offsets_ref, scale_ref, blocks_ref, retention_ref, index_ref, gain_ref,
    scale_rows_ref, readings_ref, noise_ref, start_ref, smoother_ref,
    cov_ref, smooth_ref,
    spread_ref, left_ref, right_ref, cov_now, cov_half, inject_ref, pred_ref, innov_ref,
    power_ref,
):
    segment, panel = where_ref[0], where_ref[1]
    block_count, bands, size, _ = blocks_ref.shape
    nodes = block_count * size
    frames = readings_ref.shape[0]
    own = smooth_ref.shape[0]
    width = smooth_ref.shape[1]
    segments = frames // own

    hit_t = (
        lax.broadcasted_iota(jnp.int32, (nodes, index_ref.shape[1]), 0) == index_ref[...]
    ).astype(F32)
    gained = hit_t * gain_ref[...]
    damp_col = 1.0 - jnp.sum(gained, axis=1, keepdims=True)
    damp_row = 1.0 - jnp.sum(jnp.transpose(gained), axis=0, keepdims=True)
    inverse_damp = 1.0 / damp_row
    inject_ref[...] = lax.dot_general(
        readings_ref[...] * gain_ref[...], hit_t, NT,
        precision=lax.Precision.HIGHEST, preferred_element_type=F32,
    )

    keep_col = column(retention_ref[...])
    for row in range(block_count):
        rows = slice(row * size, (row + 1) * size)
        parts = [blocks_ref[row, band] for band in range(bands)]
        total = jnp.sum(functools.reduce(jnp.add, parts), axis=1, keepdims=True)
        factor = damp_col[rows] * (1.0 - keep_col[rows, :1]) / total
        parts = [part * factor for part in parts]
        for col in range(block_count):
            placed = jnp.zeros((size, size), F32)
            for band in range(bands):
                placed += jnp.where(offsets_ref[row, band] == col, parts[band], 0.0)
            spread_ref[rows, col * size : (col + 1) * size] = placed
    left_ref[...] = spread_ref[...].astype(BF16)
    right_ref[...] = jnp.transpose(spread_ref[...]).astype(BF16)
    diag_row = damp_row * retention_ref[...]
    diag_col = column(diag_row)[:, :1]

    extra = cov_half.shape[0] - nodes
    extra_row = lax.broadcasted_iota(jnp.int32, (extra, nodes), 0)

    def mean_rows(mean):
        low = mean - mean.astype(BF16).astype(F32)
        return jnp.where(extra_row == 0, mean, jnp.where(extra_row == 1, low, 0.0)).astype(BF16)

    def mean_step(frame, mean, spread_mean):
        scale_row = scale_rows_ref[pl.ds(frame, 1), :]
        moved = scale_row * (diag_row * mean + spread_mean)
        pred = moved * inverse_damp
        mean = moved + inject_ref[pl.ds(frame, 1), :]
        pred_ref[pl.ds(frame, 1), :] = pred
        innov_ref[pl.ds(frame, 1), :] = mean - pred
        return mean

    cov_now[...] = jnp.zeros_like(cov_now)
    cov_half[...] = jnp.zeros_like(cov_half)
    chunk = 256
    chunks = [slice(at, at + chunk) for at in range(0, nodes, chunk)]

    def full_frame(frame, mean):
        cov_half[nodes:, :] = mean_rows(mean)
        half = cov_half[...]
        firsts = []
        spread_mean = []
        for cols in chunks:
            product = dot(half, right_ref[:, cols])
            firsts.append(product[:nodes] + cov_now[:, cols] * diag_row[:, cols])
            spread_mean.append(product[nodes : nodes + 1] + product[nodes + 1 : nodes + 2])
        for cols, first in zip(chunks, firsts):
            second = dot(left_ref[...], first.astype(BF16)) + diag_col * first
            scale_row = scale_rows_ref[pl.ds(frame, 1), cols]
            for row in range(block_count):
                rows = slice(row * size, (row + 1) * size)
                both = scale_row * scale_ref[frame, row]
                value = second[rows] * both + noise_ref[rows, cols]
                cov_now[rows, cols] = value
                cov_half[rows, cols] = value.astype(BF16)
        return mean_step(frame, mean, jnp.concatenate(spread_mean, axis=1))

    def mean_frame(frame, mean):
        product = dot(mean_rows(mean), right_ref[...])
        return mean_step(frame, mean, product[0:1] + product[1:2])

    def segment_of(step):
        def body(index, mean):
            for offset in range(own):
                mean = step(index * own + offset, mean)
            return mean

        return body

    mean = lax.fori_loop(0, segment + 1, segment_of(full_frame), start_ref[...])
    cov_ref[0] = cov_now[:, pl.ds(pl.multiple_of(panel * width, width), width)]
    lax.fori_loop(segment + 1, segments, segment_of(mean_frame), mean)

    innov_ref[frames:, :] = jnp.zeros((frames, nodes), F32)
    power_ref[...] = smoother_ref[...]
    step = 1
    while step < frames:
        high, low = split(power_ref[...])
        later_high, later_low = split(innov_ref[pl.ds(step, frames), :])
        moved = dot_nt(later_high, high) + (dot_nt(later_high, low) + dot_nt(later_low, high))
        innov_ref[:frames, :] = innov_ref[:frames, :] + moved
        step *= 2
        if step < frames:
            power_ref[...] = dot(high, high) + (dot(high, low) + dot(low, high))
    lanes = pl.ds(pl.multiple_of(panel * width, width), width)
    for offset in range(own):
        at = pl.ds(segment * own + offset, 1)
        smooth_ref[offset : offset + 1, :] = pred_ref[at, lanes] + innov_ref[at, lanes]


def local(
    band_blocks,
    band_offsets,
    retention,
    frame_scale,
    sensor_index,
    sensor_gain,
    readings,
    noise_cov,
    initial_mean,
    smoother_gain,
):
    nodes = retention.shape[0]
    size = band_blocks.shape[2]
    own = readings.shape[0]
    width = noise_cov.shape[1]
    scales = lax.all_gather(frame_scale, "tm", axis=0, tiled=True)
    all_readings = lax.all_gather(readings, "tm", axis=0, tiled=True)
    noise = lax.all_gather(noise_cov, "rows", axis=1, tiled=True)
    frames = scales.shape[0]
    where = jnp.stack([lax.axis_index("tm"), lax.axis_index("rows")]).astype(jnp.int32)
    smem = pl.BlockSpec(memory_space=pltpu.SMEM)
    vmem = pl.BlockSpec(memory_space=pltpu.VMEM)
    return pl.pallas_call(
        kernel,
        out_shape=(
            jax.ShapeDtypeStruct((1, nodes, width), F32),
            jax.ShapeDtypeStruct((own, width), F32),
        ),
        in_specs=[smem] * 3 + [vmem] * 9,
        out_specs=(vmem, vmem),
        scratch_shapes=[
            pltpu.VMEM((nodes, nodes), F32),
            pltpu.VMEM((nodes, nodes), BF16),
            pltpu.VMEM((nodes, nodes), BF16),
            pltpu.VMEM((nodes, nodes), F32),
            pltpu.VMEM((nodes + 16, nodes), BF16),
            pltpu.VMEM((frames, nodes), F32),
            pltpu.VMEM((frames, nodes), F32),
            pltpu.VMEM((2 * frames, nodes), F32),
            pltpu.VMEM((nodes, nodes), F32),
        ],
        compiler_params=pltpu.CompilerParams(vmem_limit_bytes=48 * 1024 * 1024),
    )(
        where, band_offsets, scales, band_blocks, retention[None], sensor_index[None],
        sensor_gain[None], jnp.repeat(scales, size, axis=1), all_readings, noise,
        initial_mean[None], smoother_gain,
    )


def solution(mesh):
    return jax.shard_map(
        local,
        mesh=mesh,
        in_specs=(P(), P(), P(), P("tm", None), P(), P(), P("tm", None), P(None, "rows"), P(), P()),
        out_specs=(P("tm", None, "rows"), P("tm", "rows")),
        check_vma=False,
    )
```

profile of v0, /device:TPU:30, one launch (start us, length us, event | category | flops | bytes accessed | tf_op | source)
XLA Modules:
  0.0 151.7 jit_solution(12172162144512550838)
XLA Ops:
  7.2 0.0 copy-start
  7.2 0.0 all-gather.4.cloned.1.call-start
  7.2 0.7 all-gather.4.cloned.1.call-update
  7.9 0.8 copy.13.offsets_ref
  8.7 35.6 %all-gather = f32[16,4,8]{2,1,0:T(4,128)S(1)} all-gather(f32[1,4,8]{2,1,0:T(4,128)} %bitcast.17), channel_id=1, replica_groups=mesh['tm'=16,'rows'=2] {'tm'}, dimensions={0}, use_global_device_ids=true | all-gather | bytes 2176 | tf_op jit(solution)/shard_map/all_gather | solution.py:166
  44.3 0.1 broadcast_in_dim.18
  44.4 0.0 copy-start.7
  44.4 0.1 reshape.7.scale_rows_ref
  44.5 0.6 copy-done.7
  45.1 37.9 %all-gather.1 = f32[16,4,128]{2,1,0:T(4,128)S(1)} all-gather(f32[1,4,128]{2,1,0:T(4,128)S(1)} %bitcast.18), channel_id=1, replica_groups=mesh['tm'=16,'rows'=2] {'tm'}, dimensions={0}, use_global_device_ids=true | all-gather | bytes 34816 | tf_op jit(solution)/shard_map/all_gather | solution.py:167
  83.0 0.1 pad_add_fusion.where_ref
  83.0 0.0 all-gather.4.cloned.1.call-done.noise_ref
  83.0 0.0 copy-start.4
  83.0 0.0 copy-start.3
  83.0 0.0 copy-start.5
  83.0 0.0 copy-start.6
  83.1 0.0 copy-done
  83.1 0.7 copy-done.4
  83.7 0.0 copy-done.3
  83.7 0.0 copy-done.5
  83.7 0.0 copy-done.6
  83.7 0.0 copy-start.1
  83.7 1.2 copy-done.1
  85.0 0.0 copy-start.2
  85.0 1.1 copy-done.2
  86.1 58.7 %shard_map.113 = (f32[1,512,256]{2,1,0:T(8,128)}, f32[4,256]{1,0:T(4,128)}) custom-call(s32[2]{0:T(128)S(1)} %pad_add_fusion.where_ref, s32[8,3]{1,0:T(8,128)S(1)} %copy.13.offsets_ref, f32[64,8]{1,0:T(8,128)S(1)} %bitcast.11, f32[8,3,64,64]{3,2,1,0:T(8,128)S(1)} %copy-done.2, f32[1,512]{1,0:T(1,128)S(1)} %bitcast.13, s32[1,128]{1,0:T(1,128)S(1)} %bitcast.15, ...), custom_call_target="tpu_custom_call" | custom-call | tf_op jit(solution)/shard_map/pallas_call | solution.py:173
Async XLA Ops:
  7.2 75.9 %copy-start = (f32[512,512]{1,0:T(8,128)S(1)}, f32[512,512]{1,0:T(8,128)}, u32[]{:S(2)}) copy-start(f32[512,512]{1,0:T(8,128)} %smoother_ref.1) | copy-start | bytes 3145732
  7.2 75.9 %all-gather.4.cloned.1.call-start = ((), (), s32[]{:S(2)}) async-start(), calls=%async_computation | async-start | bytes 1572864 | tf_op jit(solution)/shard_map/all_gather | solution.py:168
  44.4 0.7 copy-start.7
  83.0 0.7 copy-start.4
  83.0 0.7 copy-start.3
  83.0 0.7 copy-start.5
  83.0 0.7 copy-start.6
  83.7 1.2 copy-start.1
  85.0 1.1 copy-start.2
Sparse Core Ops, SparseCore 0:
  9.6 10.1 all-gather.3
where the time goes:
time: 152 us
  blocking collectives  73.5 us (48%)
  Pallas kernels  58.7 us (39%)
  between operations  14.1 us (9%)
  local copies, waits for them, and re-layouts  4.6 us (3%)
    pallas_call x1, Pallas kernels, local(): pl.pallas_call(kernel, out_shape=(jax.ShapeDtypeStruct((1, nodes, width),...  58.7 us
    all_gather x1, blocking collectives, local(): all_readings = lax.all_gather(readings, 'tm', axis=0, tiled=True)  37.9 us
    all_gather x1, blocking collectives, local(): scales = lax.all_gather(frame_scale, 'tm', axis=0, tiled=True)  35.6 us
    unnamed x17, local copies, waits for them, and re-layouts  4.36 us
  transfers between devices with their start and end apart: 1, of which 0 were waited for; matrix products, arithmetic and copies ran while one was open for 1% of the time, Pallas kernels for 0%

commit v1 on v0

--- a/solution.py
+++ b/solution.py
@@ -27,6 +27,79 @@
 
 def column(row, width=128):
     return jnp.transpose(jnp.broadcast_to(row, (width, row.shape[1])))
+
+
+def gather_kernel(
+    scale_ref, readings_ref, noise_ref,
+    scales_ref, scale_rows_ref, all_readings_ref, whole_noise_ref,
+    packed, landed, panels, send_sems, recv_sems, panel_sems,
+):
+    segment, panel = lax.axis_index("tm"), lax.axis_index("rows")
+    segments = landed.shape[0]
+    own, sensors = readings_ref.shape
+    count = scale_ref.shape[1]
+    width = noise_ref.shape[1]
+    mesh_id = pl.DeviceIdType.MESH
+
+    barrier = pltpu.get_barrier_semaphore()
+    pl.semaphore_signal(barrier, inc=1, device_id=(segment, 1 - panel), device_id_type=mesh_id)
+
+    def greet(step, carry):
+        peer = lax.rem(segment + step, segments)
+        pl.semaphore_signal(barrier, inc=1, device_id=(peer, panel), device_id_type=mesh_id)
+        return carry
+
+    lax.fori_loop(1, segments, greet, 0)
+    packed[...] = jnp.zeros_like(packed)
+    packed[:, :sensors] = readings_ref[...]
+    packed[:, sensors : sensors + count] = scale_ref[...]
+    pl.semaphore_wait(barrier, segments)
+
+    def panel_copy():
+        return pltpu.make_async_remote_copy(
+            src_ref=noise_ref, dst_ref=panels, send_sem=panel_sems.at[0],
+            recv_sem=panel_sems.at[1], device_id=(segment, 1 - panel), device_id_type=mesh_id,
+        )
+
+    def segment_copy(peer, slot, sem):
+        return pltpu.make_async_remote_copy(
+            src_ref=packed, dst_ref=landed.at[slot], send_sem=send_sems.at[sem],
+            recv_sem=recv_sems.at[slot], device_id=(peer, panel), device_id_type=mesh_id,
+        )
+
+    def send(step, carry):
+        segment_copy(lax.rem(segment + step, segments), segment, step).start()
+        return carry
+
+    lax.fori_loop(1, segments, send, 0)
+    panel_copy().start()
+    landed[segment] = packed[...]
+    whole_noise_ref[:, pl.ds(pl.multiple_of(panel * width, width), width)] = noise_ref[...]
+
+    def arrive(step, carry):
+        source = lax.rem(segment + step, segments)
+        copy = segment_copy(source, source, step)
+        copy.wait_recv()
+        copy.wait_send()
+        return carry
+
+    lax.fori_loop(1, segments, arrive, 0)
+    for index in range(segments):
+        rows = slice(index * own, (index + 1) * own)
+        got = landed[index]
+        all_readings_ref[rows, :] = got[:, :sensors]
+        scales = got[:, sensors : sensors + count]
+        scales_ref[rows, :] = scales
+        nodes = scale_rows_ref.shape[1]
+        block = lax.broadcasted_iota(jnp.int32, (own, nodes), 1) // (nodes // count)
+        spread = jnp.zeros((own, nodes), F32)
+        for col in range(count):
+            spread = jnp.where(block == col, scales[:, col : col + 1], spread)
+        scale_rows_ref[rows, :] = spread
+    copy = panel_copy()
+    copy.wait_recv()
+    copy.wait_send()
+    whole_noise_ref[:, pl.ds(pl.multiple_of((1 - panel) * width, width), width)] = panels[...]
 
 
 def kernel(
@@ -71,7 +144,8 @@
     left_ref[...] = spread_ref[...].astype(BF16)
     right_ref[...] = jnp.transpose(spread_ref[...]).astype(BF16)
     diag_row = damp_row * retention_ref[...]
-    diag_col = column(diag_row)[:, :1]
+    diag_col = column(diag_row)
+    diag_col = jnp.concatenate([diag_col, diag_col], axis=1)
 
     extra = cov_half.shape[0] - nodes
     extra_row = lax.broadcasted_iota(jnp.int32, (extra, nodes), 0)
@@ -89,8 +163,6 @@
         innov_ref[pl.ds(frame, 1), :] = mean - pred
         return mean
 
-    cov_now[...] = jnp.zeros_like(cov_now)
-    cov_half[...] = jnp.zeros_like(cov_half)
     chunk = 256
     chunks = [slice(at, at + chunk) for at in range(0, nodes, chunk)]
 
@@ -126,21 +198,33 @@
 
         return body
 
-    mean = lax.fori_loop(0, segment + 1, segment_of(full_frame), start_ref[...])
+    mean = mean_frame(0, start_ref[...])
+    cov_now[...] = noise_ref[...]
+    cov_half[:nodes, :] = noise_ref[...].astype(BF16)
+    mean = lax.fori_loop(1, own, full_frame, mean)
+    mean = lax.fori_loop(1, segment + 1, segment_of(full_frame), mean)
     cov_ref[0] = cov_now[:, pl.ds(pl.multiple_of(panel * width, width), width)]
     lax.fori_loop(segment + 1, segments, segment_of(mean_frame), mean)
 
     innov_ref[frames:, :] = jnp.zeros((frames, nodes), F32)
     power_ref[...] = smoother_ref[...]
+    left = frames - segment * own
+
+    def double(step):
+        later_high, later_low = split(innov_ref[pl.ds(step, frames), :])
+        if step > 1:
+            before_high, before_low = split(power_ref[...])
+            power_ref[...] = dot(before_high, before_high) + (
+                dot(before_high, before_low) + dot(before_low, before_high)
+            )
+        high, low = split(power_ref[...])
+        moved = dot_nt(later_high, high) + (dot_nt(later_high, low) + dot_nt(later_low, high))
+        innov_ref[:frames, :] = innov_ref[:frames, :] + moved
+
     step = 1
     while step < frames:
-        high, low = split(power_ref[...])
-        later_high, later_low = split(innov_ref[pl.ds(step, frames), :])
-        moved = dot_nt(later_high, high) + (dot_nt(later_high, low) + dot_nt(later_low, high))
-        innov_ref[:frames, :] = innov_ref[:frames, :] + moved
+        pl.when(step < left)(functools.partial(double, step))
         step *= 2
-        if step < frames:
-            power_ref[...] = dot(high, high) + (dot(high, low) + dot(low, high))
     lanes = pl.ds(pl.multiple_of(panel * width, width), width)
     for offset in range(own):
         at = pl.ds(segment * own + offset, 1)
@@ -160,16 +244,38 @@
     smoother_gain,
 ):
     nodes = retention.shape[0]
-    size = band_blocks.shape[2]
     own = readings.shape[0]
     width = noise_cov.shape[1]
-    scales = lax.all_gather(frame_scale, "tm", axis=0, tiled=True)
-    all_readings = lax.all_gather(readings, "tm", axis=0, tiled=True)
-    noise = lax.all_gather(noise_cov, "rows", axis=1, tiled=True)
+    segments = lax.axis_size("tm")
+    vmem = pl.BlockSpec(memory_space=pltpu.VMEM)
+    total = segments * own
+    sensors = readings.shape[1]
+    packed_width = sensors + 128
+    scales, scale_rows, all_readings, noise = pl.pallas_call(
+        gather_kernel,
+        out_shape=(
+            jax.ShapeDtypeStruct((total, frame_scale.shape[1]), F32),
+            jax.ShapeDtypeStruct((total, nodes), F32),
+            jax.ShapeDtypeStruct((total, sensors), F32),
+            jax.ShapeDtypeStruct((nodes, nodes), F32),
+        ),
+        in_specs=[vmem] * 3,
+        out_specs=(vmem,) * 4,
+        scratch_shapes=[
+            pltpu.VMEM((own, packed_width), F32),
+            pltpu.VMEM((segments, own, packed_width), F32),
+            pltpu.VMEM((nodes, width), F32),
+            pltpu.SemaphoreType.DMA((segments,)),
+            pltpu.SemaphoreType.DMA((segments,)),
+            pltpu.SemaphoreType.DMA((2,)),
+        ],
+        compiler_params=pltpu.CompilerParams(
+            collective_id=0, has_side_effects=True, vmem_limit_bytes=16 * 1024 * 1024
+        ),
+    )(frame_scale, readings, noise_cov)
     frames = scales.shape[0]
     where = jnp.stack([lax.axis_index("tm"), lax.axis_index("rows")]).astype(jnp.int32)
     smem = pl.BlockSpec(memory_space=pltpu.SMEM)
-    vmem = pl.BlockSpec(memory_space=pltpu.VMEM)
     return pl.pallas_call(
         kernel,
         out_shape=(
@@ -192,7 +298,7 @@
         compiler_params=pltpu.CompilerParams(vmem_limit_bytes=48 * 1024 * 1024),
     )(
         where, band_offsets, scales, band_blocks, retention[None], sensor_index[None],
-        sensor_gain[None], jnp.repeat(scales, size, axis=1), all_readings, noise,
+        sensor_gain[None], scale_rows, all_readings, noise,
         initial_mean[None], smoother_gain,
     )
 

time: 152 us -> 66.4 us (0.44)
  blocking collectives: 73.5 us -> 0 us
  between operations: 14.1 us -> 0.68 us
    all_gather x2 -> x0, blocking collectives: 73.5 us -> none  [the longest x1 37.9 us: local(): all_readings = lax.all_gather(readings, 'tm', axis=0, tiled=True)]
    pallas_call x0 -> x1, Pallas kernels: none -> 8.44 us  [local(): pl.pallas_call(gather_kernel, out_shape=(jax.ShapeDtypeStruct((total, fra...]
    pallas_call x1, Pallas kernels: 58.7 us -> 51.5 us  [local(): pl.pallas_call(kernel, out_shape=(jax.ShapeDtypeStruct((1, nodes, width),...]
    unnamed x17 -> x21, local copies, waits for them, and re-layouts: 4.36 us -> 5.45 us
  transfers between devices with their start and end apart: 1 -> 0, of which waited for: 0 -> 0; matrix products, arithmetic and copies ran while one was open for 1% -> 0% of each run, Pallas kernels for 0% -> 0%
where the time goes in v1:
time: 66.4 us; the launch traced here: 66.1 us
  Pallas kernels  59.9 us (90%)
  local copies, waits for them, and re-layouts  5.45 us (8%)
  between operations  0.68 us (1%)
    pallas_call x1, Pallas kernels, local(): pl.pallas_call(kernel, out_shape=(jax.ShapeDtypeStruct((1, nodes, width),...  51.5 us
    pallas_call x1, Pallas kernels, local(): pl.pallas_call(gather_kernel, out_shape=(jax.ShapeDtypeStruct((total, fra...  8.44 us
    unnamed x21, local copies, waits for them, and re-layouts  5.45 us

profile of v1, /device:TPU:30, one launch (start us, length us, event | category | flops | bytes accessed | tf_op | source)
XLA Modules:
  0.0 66.1 jit_solution(15402471005821807997)
XLA Ops:
  0.6 0.1 pad_add_fusion.where_ref
  0.7 0.0 copy-start.9
  0.7 0.7 %copy-done.9 = s32[8,3]{0,1:T(4,128)S(1)} copy-done((s32[8,3]{0,1:T(4,128)S(1)}, s32[8,3]{0,1:T(4,128)}, u32[]{:S(2)}) %copy-start.9) | copy-done | bytes 120
  1.4 0.0 copy-start.3
  1.4 0.0 copy-start.4
  1.4 0.1 copy.12.offsets_ref
  1.5 0.6 copy-done.3
  2.1 0.0 copy-done.4
  2.1 0.0 copy-start.2
  2.1 1.0 %copy-done.2 = f32[512,256]{1,0:T(8,128)S(1)} copy-done((f32[512,256]{1,0:T(8,128)S(1)}, f32[512,256]{1,0:T(8,128)}, u32[]{:S(2)}) %copy-start.2) | copy-done | bytes 524312
  3.1 8.4 %shard_map.113 = (f32[64,8]{1,0:T(8,128)S(1)}, f32[64,512]{1,0:T(8,128)S(1)}, f32[64,128]{1,0:T(8,128)S(1)}, f32[512,512]{1,0:T(8,128)S(1)}) custom-call(f32[4,8]{1,0:T(4,128)S(1)} %copy-done.3, f32[4,128]{1,0:T(4,128)S(1)} %copy-done.4, f32[512,256]{1,0:T(8,128)S(1)} %copy-done.2), custom_call_target="tpu_custom_call" | custom-call | tf_op jit(solution)/shard_map/pallas_call | solution.py:254
  11.6 0.0 copy-start.6
  11.6 0.0 copy-start.5
  11.6 0.0 copy-start.7
  11.6 0.0 copy-start.8
  11.6 0.6 copy-done.6
  12.3 0.0 copy-done.5
  12.3 0.0 copy-done.7
  12.3 0.0 copy-done.8
  12.3 0.0 copy-start
  12.3 1.2 %copy-done = f32[512,512]{1,0:T(8,128)S(1)} copy-done((f32[512,512]{1,0:T(8,128)S(1)}, f32[512,512]{1,0:T(8,128)}, u32[]{:S(2)}) %copy-start) | copy-done | bytes 1048600
  13.5 0.0 copy-start.1
  13.5 1.1 %copy-done.1 = f32[8,3,64,64]{3,2,1,0:T(8,128)S(1)} copy-done((f32[8,3,64,64]{3,2,1,0:T(8,128)S(1)}, f32[8,3,64,64]{3,2,1,0:T(8,128)}, u32[]{:S(2)}) %copy-start.1) | copy-done | bytes 393240
  14.6 51.5 %shard_map.114 = (f32[1,512,256]{2,1,0:T(8,128)}, f32[4,256]{1,0:T(4,128)}) custom-call(s32[2]{0:T(128)S(1)} %pad_add_fusion.where_ref, s32[8,3]{1,0:T(8,128)S(1)} %copy.12.offsets_ref, f32[64,8]{1,0:T(8,128)S(1)} %get-tuple-element.6.scale_ref, f32[8,3,64,64]{3,2,1,0:T(8,128)S(1)} %copy-done.1, f32[1,512]{1,0:T(1,128)S(1)} %bitcast.6, ...), custom_call_target="tpu_custom_call" | custom-call | tf_op jit(solution)/shard_map/pallas_call | solution.py:279
Async XLA Ops:
  0.7 0.7 %copy-start.9 = (s32[8,3]{0,1:T(4,128)S(1)}, s32[8,3]{0,1:T(4,128)}, u32[]{:S(2)}) copy-start(s32[8,3]{0,1:T(4,128)} %param.11) | copy-start | bytes 292
  1.4 0.7 %copy-start.3 = (f32[4,8]{1,0:T(4,128)S(1)}, f32[4,8]{1,0:T(4,128)}, u32[]{:S(2)}) copy-start(f32[4,8]{1,0:T(4,128)} %scale_ref.1) | copy-start | bytes 388
  1.4 0.7 %copy-start.4 = (f32[4,128]{1,0:T(4,128)S(1)}, f32[4,128]{1,0:T(4,128)}, u32[]{:S(2)}) copy-start(f32[4,128]{1,0:T(4,128)} %readings_ref.1) | copy-start | bytes 6148
  2.1 1.0 %copy-start.2 = (f32[512,256]{1,0:T(8,128)S(1)}, f32[512,256]{1,0:T(8,128)}, u32[]{:S(2)}) copy-start(f32[512,256]{1,0:T(8,128)} %noise_ref.1) | copy-start | bytes 1572868
  11.6 0.7 %copy-start.6 = (f32[512]{0:T(512)S(1)}, f32[512]{0:T(512)}, u32[]{:S(2)}) copy-start(f32[512]{0:T(512)} %param.18) | copy-start | bytes 6148
  11.6 0.7 %copy-start.5 = (f32[512]{0:T(512)S(1)}, f32[512]{0:T(512)}, u32[]{:S(2)}) copy-start(f32[512]{0:T(512)} %param.12) | copy-start | bytes 6148
  11.6 0.7 %copy-start.7 = (s32[128]{0:T(128)S(1)}, s32[128]{0:T(128)}, u32[]{:S(2)}) copy-start(s32[128]{0:T(128)} %param.14) | copy-start | bytes 1540
  11.6 0.7 %copy-start.8 = (f32[128]{0:T(128)S(1)}, f32[128]{0:T(128)}, u32[]{:S(2)}) copy-start(f32[128]{0:T(128)} %param.15) | copy-start | bytes 1540
  12.3 1.2 %copy-start = (f32[512,512]{1,0:T(8,128)S(1)}, f32[512,512]{1,0:T(8,128)}, u32[]{:S(2)}) copy-start(f32[512,512]{1,0:T(8,128)} %smoother_ref.1) | copy-start | bytes 3145732
  13.5 1.1 %copy-start.1 = (f32[8,3,64,64]{3,2,1,0:T(8,128)S(1)}, f32[8,3,64,64]{3,2,1,0:T(8,128)}, u32[]{:S(2)}) copy-start(f32[8,3,64,64]{3,2,1,0:T(8,128)} %blocks_ref.1) | copy-start | bytes 1179652

commit v2 on v1

--- a/solution.py
+++ b/solution.py
@@ -107,7 +107,7 @@
     scale_rows_ref, readings_ref, noise_ref, start_ref, smoother_ref,
     cov_ref, smooth_ref,
     spread_ref, left_ref, right_ref, cov_now, cov_half, inject_ref, pred_ref, innov_ref,
-    power_ref,
+    power_ref, smoother_sem,
 ):
     segment, panel = where_ref[0], where_ref[1]
     block_count, bands, size, _ = blocks_ref.shape
@@ -116,6 +116,9 @@
     own = smooth_ref.shape[0]
     width = smooth_ref.shape[1]
     segments = frames // own
+
+    smoother_copy = pltpu.make_async_copy(smoother_ref, power_ref, smoother_sem)
+    smoother_copy.start()
 
     hit_t = (
         lax.broadcasted_iota(jnp.int32, (nodes, index_ref.shape[1]), 0) == index_ref[...]
@@ -207,7 +210,7 @@
     lax.fori_loop(segment + 1, segments, segment_of(mean_frame), mean)
 
     innov_ref[frames:, :] = jnp.zeros((frames, nodes), F32)
-    power_ref[...] = smoother_ref[...]
+    smoother_copy.wait()
     left = frames - segment * own
 
     def double(step):
@@ -282,7 +285,7 @@
             jax.ShapeDtypeStruct((1, nodes, width), F32),
             jax.ShapeDtypeStruct((own, width), F32),
         ),
-        in_specs=[smem] * 3 + [vmem] * 9,
+        in_specs=[smem] * 3 + [vmem] * 8 + [pl.BlockSpec(memory_space=pl.ANY)],
         out_specs=(vmem, vmem),
         scratch_shapes=[
             pltpu.VMEM((nodes, nodes), F32),
@@ -294,6 +297,7 @@
             pltpu.VMEM((frames, nodes), F32),
             pltpu.VMEM((2 * frames, nodes), F32),
             pltpu.VMEM((nodes, nodes), F32),
+            pltpu.SemaphoreType.DMA,
         ],
         compiler_params=pltpu.CompilerParams(vmem_limit_bytes=48 * 1024 * 1024),
     )(

time: 66.4 us -> 66.4 us (level)
  no operation moved by 1% of the time
where the time goes in v2:
time: 66.4 us; the launch traced here: 66.1 us
  Pallas kernels  59.9 us (90%)
  local copies, waits for them, and re-layouts  5.45 us (8%)
  between operations  0.68 us (1%)
    pallas_call x1, Pallas kernels, local(): pl.pallas_call(kernel, out_shape=(jax.ShapeDtypeStruct((1, nodes, width),...  51.5 us
    pallas_call x1, Pallas kernels, local(): pl.pallas_call(gather_kernel, out_shape=(jax.ShapeDtypeStruct((total, fra...  8.44 us
    unnamed x21, local copies, waits for them, and re-layouts  5.45 us

profile of v2, /device:TPU:30, one launch (start us, length us, event | category | flops | bytes accessed | tf_op | source)
XLA Modules:
  0.0 66.1 jit_solution(5056714669015525115)
XLA Ops:
  0.6 0.1 pad_add_fusion.where_ref
  0.7 0.0 copy-start.9
  0.7 0.7 %copy-done.9 = s32[8,3]{0,1:T(4,128)S(1)} copy-done((s32[8,3]{0,1:T(4,128)S(1)}, s32[8,3]{0,1:T(4,128)}, u32[]{:S(2)}) %copy-start.9) | copy-done | bytes 120
  1.4 0.0 copy-start.3
  1.4 0.0 copy-start.4
  1.4 0.1 copy.12.offsets_ref
  1.5 0.6 copy-done.3
  2.1 0.0 copy-done.4
  2.1 0.0 copy-start.2
  2.1 1.0 %copy-done.2 = f32[512,256]{1,0:T(8,128)S(1)} copy-done((f32[512,256]{1,0:T(8,128)S(1)}, f32[512,256]{1,0:T(8,128)}, u32[]{:S(2)}) %copy-start.2) | copy-done | bytes 524312
  3.1 8.4 %shard_map.113 = (f32[64,8]{1,0:T(8,128)S(1)}, f32[64,512]{1,0:T(8,128)S(1)}, f32[64,128]{1,0:T(8,128)S(1)}, f32[512,512]{1,0:T(8,128)S(1)}) custom-call(f32[4,8]{1,0:T(4,128)S(1)} %copy-done.3, f32[4,128]{1,0:T(4,128)S(1)} %copy-done.4, f32[512,256]{1,0:T(8,128)S(1)} %copy-done.2), custom_call_target="tpu_custom_call" | custom-call | tf_op jit(solution)/shard_map/pallas_call | solution.py:257
  11.6 0.0 copy-start.6
  11.6 0.0 copy-start.5
  11.6 0.0 copy-start.7
  11.6 0.0 copy-start.8
  11.6 0.6 copy-done.6
  12.3 0.0 copy-done.5
  12.3 0.0 copy-done.7
  12.3 0.0 copy-done.8
  12.3 0.0 copy-start
  12.3 1.2 %copy-done = f32[512,512]{1,0:T(8,128)S(1)} copy-done((f32[512,512]{1,0:T(8,128)S(1)}, f32[512,512]{1,0:T(8,128)}, u32[]{:S(2)}) %copy-start) | copy-done | bytes 1048600
  13.5 0.0 copy-start.1
  13.5 1.1 %copy-done.1 = f32[8,3,64,64]{3,2,1,0:T(8,128)S(1)} copy-done((f32[8,3,64,64]{3,2,1,0:T(8,128)S(1)}, f32[8,3,64,64]{3,2,1,0:T(8,128)}, u32[]{:S(2)}) %copy-start.1) | copy-done | bytes 393240
  14.6 51.5 %shard_map.114 = (f32[1,512,256]{2,1,0:T(8,128)}, f32[4,256]{1,0:T(4,128)}) custom-call(s32[2]{0:T(128)S(1)} %pad_add_fusion.where_ref, s32[8,3]{1,0:T(8,128)S(1)} %copy.12.offsets_ref, f32[64,8]{1,0:T(8,128)S(1)} %get-tuple-element.6.scale_ref, f32[8,3,64,64]{3,2,1,0:T(8,128)S(1)} %copy-done.1, f32[1,512]{1,0:T(1,128)S(1)} %bitcast.6, ...), custom_call_target="tpu_custom_call" | custom-call | tf_op jit(solution)/shard_map/pallas_call | solution.py:282
Async XLA Ops:
  0.7 0.7 %copy-start.9 = (s32[8,3]{0,1:T(4,128)S(1)}, s32[8,3]{0,1:T(4,128)}, u32[]{:S(2)}) copy-start(s32[8,3]{0,1:T(4,128)} %param.11) | copy-start | bytes 292
  1.4 0.7 %copy-start.3 = (f32[4,8]{1,0:T(4,128)S(1)}, f32[4,8]{1,0:T(4,128)}, u32[]{:S(2)}) copy-start(f32[4,8]{1,0:T(4,128)} %scale_ref.1) | copy-start | bytes 388
  1.4 0.7 %copy-start.4 = (f32[4,128]{1,0:T(4,128)S(1)}, f32[4,128]{1,0:T(4,128)}, u32[]{:S(2)}) copy-start(f32[4,128]{1,0:T(4,128)} %readings_ref.1) | copy-start | bytes 6148
  2.1 1.0 %copy-start.2 = (f32[512,256]{1,0:T(8,128)S(1)}, f32[512,256]{1,0:T(8,128)}, u32[]{:S(2)}) copy-start(f32[512,256]{1,0:T(8,128)} %noise_ref.1) | copy-start | bytes 1572868
  11.6 0.7 %copy-start.6 = (f32[512]{0:T(512)S(1)}, f32[512]{0:T(512)}, u32[]{:S(2)}) copy-start(f32[512]{0:T(512)} %param.18) | copy-start | bytes 6148
  11.6 0.7 %copy-start.5 = (f32[512]{0:T(512)S(1)}, f32[512]{0:T(512)}, u32[]{:S(2)}) copy-start(f32[512]{0:T(512)} %param.12) | copy-start | bytes 6148
  11.6 0.7 %copy-start.7 = (s32[128]{0:T(128)S(1)}, s32[128]{0:T(128)}, u32[]{:S(2)}) copy-start(s32[128]{0:T(128)} %param.14) | copy-start | bytes 1540
  11.6 0.7 %copy-start.8 = (f32[128]{0:T(128)S(1)}, f32[128]{0:T(128)}, u32[]{:S(2)}) copy-start(f32[128]{0:T(128)} %param.15) | copy-start | bytes 1540
  12.3 1.2 %copy-start = (f32[512,512]{1,0:T(8,128)S(1)}, f32[512,512]{1,0:T(8,128)}, u32[]{:S(2)}) copy-start(f32[512,512]{1,0:T(8,128)} %smoother_ref.1) | copy-start | bytes 3145732
  13.5 1.1 %copy-start.1 = (f32[8,3,64,64]{3,2,1,0:T(8,128)S(1)}, f32[8,3,64,64]{3,2,1,0:T(8,128)}, u32[]{:S(2)}) copy-start(f32[8,3,64,64]{3,2,1,0:T(8,128)} %blocks_ref.1) | copy-start | bytes 1179652

commit v3 on v2

--- a/solution.py
+++ b/solution.py
@@ -103,11 +103,11 @@
 
 
 def kernel(
-    where_ref, offsets_ref, scale_ref, blocks_ref, retention_ref, index_ref, gain_ref,
+    where_ref, offsets_ref, scale_ref, blocks_hbm, retention_ref, index_ref, gain_ref,
     scale_rows_ref, readings_ref, noise_ref, start_ref, smoother_ref,
     cov_ref, smooth_ref,
     spread_ref, left_ref, right_ref, cov_now, cov_half, inject_ref, pred_ref, innov_ref,
-    power_ref, smoother_sem,
+    power_ref, smoother_sem, blocks_ref, blocks_sem,
 ):
     segment, panel = where_ref[0], where_ref[1]
     block_count, bands, size, _ = blocks_ref.shape
@@ -117,6 +117,8 @@
     width = smooth_ref.shape[1]
     segments = frames // own
 
+    blocks_copy = pltpu.make_async_copy(blocks_hbm, blocks_ref, blocks_sem)
+    blocks_copy.start()
     smoother_copy = pltpu.make_async_copy(smoother_ref, power_ref, smoother_sem)
     smoother_copy.start()
 
@@ -132,6 +134,7 @@
         precision=lax.Precision.HIGHEST, preferred_element_type=F32,
     )
 
+    blocks_copy.wait()
     keep_col = column(retention_ref[...])
     for row in range(block_count):
         rows = slice(row * size, (row + 1) * size)
@@ -285,7 +288,7 @@
             jax.ShapeDtypeStruct((1, nodes, width), F32),
             jax.ShapeDtypeStruct((own, width), F32),
         ),
-        in_specs=[smem] * 3 + [vmem] * 8 + [pl.BlockSpec(memory_space=pl.ANY)],
+        in_specs=[smem] * 3 + [pl.BlockSpec(memory_space=pl.ANY)] + [vmem] * 7 + [pl.BlockSpec(memory_space=pl.ANY)],
         out_specs=(vmem, vmem),
         scratch_shapes=[
             pltpu.VMEM((nodes, nodes), F32),
@@ -298,6 +301,8 @@
             pltpu.VMEM((2 * frames, nodes), F32),
             pltpu.VMEM((nodes, nodes), F32),
             pltpu.SemaphoreType.DMA,
+            pltpu.VMEM(band_blocks.shape, F32),
+            pltpu.SemaphoreType.DMA,
         ],
         compiler_params=pltpu.CompilerParams(vmem_limit_bytes=48 * 1024 * 1024),
     )(

time: 66.4 us -> 66.7 us (level)
  no operation moved by 1% of the time
where the time goes in v3:
time: 66.7 us; the launch traced here: 66.4 us
  Pallas kernels  60.2 us (90%)
  local copies, waits for them, and re-layouts  5.45 us (8%)
  between operations  0.68 us (1%)
    pallas_call x1, Pallas kernels, local(): pl.pallas_call(kernel, out_shape=(jax.ShapeDtypeStruct((1, nodes, width),...  51.7 us
    pallas_call x1, Pallas kernels, local(): pl.pallas_call(gather_kernel, out_shape=(jax.ShapeDtypeStruct((total, fra...  8.44 us
    unnamed x21, local copies, waits for them, and re-layouts  5.45 us

profile of v3, /device:TPU:30, one launch (start us, length us, event | category | flops | bytes accessed | tf_op | source)
XLA Modules:
  0.0 66.4 jit_solution(894063570387325333)
XLA Ops:
  0.6 0.1 pad_add_fusion.where_ref
  0.7 0.0 copy-start.9
  0.7 0.7 %copy-done.9 = s32[8,3]{0,1:T(4,128)S(1)} copy-done((s32[8,3]{0,1:T(4,128)S(1)}, s32[8,3]{0,1:T(4,128)}, u32[]{:S(2)}) %copy-start.9) | copy-done | bytes 120
  1.4 0.0 copy-start.3
  1.4 0.0 copy-start.4
  1.4 0.1 copy.12.offsets_ref
  1.5 0.6 copy-done.3
  2.1 0.0 copy-done.4
  2.1 0.0 copy-start.2
  2.1 1.0 %copy-done.2 = f32[512,256]{1,0:T(8,128)S(1)} copy-done((f32[512,256]{1,0:T(8,128)S(1)}, f32[512,256]{1,0:T(8,128)}, u32[]{:S(2)}) %copy-start.2) | copy-done | bytes 524312
  3.1 8.4 %shard_map.113 = (f32[64,8]{1,0:T(8,128)S(1)}, f32[64,512]{1,0:T(8,128)S(1)}, f32[64,128]{1,0:T(8,128)S(1)}, f32[512,512]{1,0:T(8,128)S(1)}) custom-call(f32[4,8]{1,0:T(4,128)S(1)} %copy-done.3, f32[4,128]{1,0:T(4,128)S(1)} %copy-done.4, f32[512,256]{1,0:T(8,128)S(1)} %copy-done.2), custom_call_target="tpu_custom_call" | custom-call | tf_op jit(solution)/shard_map/pallas_call | solution.py:260
  11.6 0.0 copy-start.6
  11.6 0.0 copy-start.5
  11.6 0.0 copy-start.7
  11.6 0.0 copy-start.8
  11.6 0.6 copy-done.6
  12.3 0.0 copy-done.5
  12.3 0.0 copy-done.7
  12.3 0.0 copy-done.8
  12.3 0.0 copy-start
  12.3 1.2 %copy-done = f32[512,512]{1,0:T(8,128)S(1)} copy-done((f32[512,512]{1,0:T(8,128)S(1)}, f32[512,512]{1,0:T(8,128)}, u32[]{:S(2)}) %copy-start) | copy-done | bytes 1048600
  13.5 0.0 copy-start.1
  13.5 1.1 %copy-done.1 = f32[8,3,64,64]{3,2,1,0:T(8,128)S(1)} copy-done((f32[8,3,64,64]{3,2,1,0:T(8,128)S(1)}, f32[8,3,64,64]{3,2,1,0:T(8,128)}, u32[]{:S(2)}) %copy-start.1) | copy-done | bytes 393240
  14.6 51.7 %shard_map.114 = (f32[1,512,256]{2,1,0:T(8,128)}, f32[4,256]{1,0:T(4,128)}) custom-call(s32[2]{0:T(128)S(1)} %pad_add_fusion.where_ref, s32[8,3]{1,0:T(8,128)S(1)} %copy.12.offsets_ref, f32[64,8]{1,0:T(8,128)S(1)} %get-tuple-element.6.scale_ref, f32[8,3,64,64]{3,2,1,0:T(8,128)S(1)} %copy-done.1, f32[1,512]{1,0:T(1,128)S(1)} %bitcast.6, ...), custom_call_target="tpu_custom_call" | custom-call | tf_op jit(solution)/shard_map/pallas_call | solution.py:285
Async XLA Ops:
  0.7 0.7 %copy-start.9 = (s32[8,3]{0,1:T(4,128)S(1)}, s32[8,3]{0,1:T(4,128)}, u32[]{:S(2)}) copy-start(s32[8,3]{0,1:T(4,128)} %param.11) | copy-start | bytes 292
  1.4 0.7 %copy-start.3 = (f32[4,8]{1,0:T(4,128)S(1)}, f32[4,8]{1,0:T(4,128)}, u32[]{:S(2)}) copy-start(f32[4,8]{1,0:T(4,128)} %scale_ref.1) | copy-start | bytes 388
  1.4 0.7 %copy-start.4 = (f32[4,128]{1,0:T(4,128)S(1)}, f32[4,128]{1,0:T(4,128)}, u32[]{:S(2)}) copy-start(f32[4,128]{1,0:T(4,128)} %readings_ref.1) | copy-start | bytes 6148
  2.1 1.0 %copy-start.2 = (f32[512,256]{1,0:T(8,128)S(1)}, f32[512,256]{1,0:T(8,128)}, u32[]{:S(2)}) copy-start(f32[512,256]{1,0:T(8,128)} %noise_ref.1) | copy-start | bytes 1572868
  11.6 0.7 %copy-start.6 = (f32[512]{0:T(512)S(1)}, f32[512]{0:T(512)}, u32[]{:S(2)}) copy-start(f32[512]{0:T(512)} %param.18) | copy-start | bytes 6148
  11.6 0.7 %copy-start.5 = (f32[512]{0:T(512)S(1)}, f32[512]{0:T(512)}, u32[]{:S(2)}) copy-start(f32[512]{0:T(512)} %param.12) | copy-start | bytes 6148
  11.6 0.7 %copy-start.7 = (s32[128]{0:T(128)S(1)}, s32[128]{0:T(128)}, u32[]{:S(2)}) copy-start(s32[128]{0:T(128)} %param.14) | copy-start | bytes 1540
  11.6 0.7 %copy-start.8 = (f32[128]{0:T(128)S(1)}, f32[128]{0:T(128)}, u32[]{:S(2)}) copy-start(f32[128]{0:T(128)} %param.15) | copy-start | bytes 1540
  12.3 1.2 %copy-start = (f32[512,512]{1,0:T(8,128)S(1)}, f32[512,512]{1,0:T(8,128)}, u32[]{:S(2)}) copy-start(f32[512,512]{1,0:T(8,128)} %smoother_ref.1) | copy-start | bytes 3145732
  13.5 1.1 %copy-start.1 = (f32[8,3,64,64]{3,2,1,0:T(8,128)S(1)}, f32[8,3,64,64]{3,2,1,0:T(8,128)}, u32[]{:S(2)}) copy-start(f32[8,3,64,64]{3,2,1,0:T(8,128)} %blocks_hbm.1) | copy-start | bytes 1179652
